TPU v7x, 512 devices: a whole 4x8x8 slice. The times are simulated.
512 devices in a mesh: dp: 16 (over z, core), fsdp: 4 (over x), tensor: 8 (over y).
Axes of the slice: x: 4, y: 8, z: 8, core: 2. Of those that a mesh axis runs over, the one named last changes fastest.
Arguments:
- tokens: bfloat16 [16384, 8192], P(('dp', 'fsdp'), 'tensor'), may hold values from -700 to 700
- queries: bfloat16 [16384, 8192], P(('dp', 'fsdp'), 'tensor'), may hold values from -140 to 140
- segment_ids: int32 [128, 128], P(('dp', 'fsdp')), may hold values from 0 to 3, never falling along the last dimension, each value on 1 to 64 neighbouring positions
- gain: float32 [8192], P('tensor'), may hold values from 0.1 to 1.9
- key_value_weight: bfloat16 [8192, 2048], P('tensor', 'fsdp'), may hold values from -0.0625 to 0.0625
- plan: int32 [32], replicated, may hold values from 0 to 31, as said below
Outputs:
- attended: bfloat16 [16384, 8192], P(('dp', 'fsdp'), 'tensor')
Inputs may be any that keep to these rules, and one draw needn't show every extreme that they name: plan is a permutation of 0 to 31; from one dp index to another at most 1 micro-batches go, and in every draw some pair of dp indices carries exactly 1.
All inputs are finite; a program needn't handle non-finite values.
Results may differ from a plain program's by a relative error of at most 0.011.
Values may be sent and summed in bfloat16 or wider, within the bound.
No kernel may reach another device: no remote copies, remote signals or barrier semaphores. Data moves between devices by JAX's collectives and lax.ppermute only.
A program may use at most 64 MiB of HBM per device.

v0:
```python
import jax
import jax.numpy as jnp
from jax import lax
from jax.sharding import PartitionSpec as P

HEAD_SIZE = 128


epsilon = 1e-05


def total_of_pieces(array, axis):
    parts = lax.all_gather(array, axis)
    return parts.sum(axis=0)


def pack_rows(send_index, send_valid, flat_rows, length):
    ranks_here = send_index.shape[0]
    slots_here = send_index.shape[1]
    taken = jnp.take(flat_rows, send_index.reshape(-1), axis=0)
    sent = taken * send_valid.astype(flat_rows.dtype)
    return sent.reshape(ranks_here, slots_here, length, -1)


def unpack_rows(keep_index, arrived):
    flat = arrived.reshape(arrived.shape[0] * arrived.shape[1], -1)
    return jnp.take(flat, keep_index, axis=0)


def project(rows, gain, key_value_weight):
    values = rows.astype(jnp.float32)
    stats = total_of_pieces(jnp.sum(values * values, axis=1), "tensor")
    full_width = rows.shape[1] * lax.axis_size("tensor")
    scale = lax.rsqrt(stats / full_width + epsilon)
    normed = (values * scale[:, None] * gain).astype(jnp.bfloat16)
    partial_value = jnp.dot(
        normed,
        lax.all_gather(key_value_weight, "fsdp", axis=1, tiled=True),
        preferred_element_type=jnp.float32,
    )
    return lax.psum_scatter(partial_value, "tensor", scatter_dimension=1, tiled=True)


def attend(query_row_block, key_value_rows, documents):
    batches, length = documents.shape
    heads_kv = key_value_rows.shape[1] // (2 * HEAD_SIZE)
    head_group = query_row_block.shape[1] // (heads_kv * HEAD_SIZE)
    query_head_count = query_row_block.astype(jnp.float32).reshape(
        batches, length, heads_kv, head_group, HEAD_SIZE
    )
    key_value_heads = key_value_rows.reshape(batches, length, heads_kv, 2, HEAD_SIZE)
    scores = jnp.einsum(
        "mqhgd,mkhd->mhgqk",
        query_head_count,
        key_value_heads[:, :, :, 0],
        precision=lax.Precision.HIGHEST,
    ) * HEAD_SIZE ** (-0.5)
    positions = jnp.arange(length, dtype=jnp.int32)
    causal = positions[:, None] >= positions[None, :]
    allowed = (documents[:, :, None] == documents[:, None, :]) & causal[None]
    scores = jnp.where(allowed[:, None, None], scores, -1e30)
    row_max = jnp.max(scores, axis=-1, keepdims=True)
    expo = jnp.exp(scores - row_max)
    weights = (expo / jnp.sum(expo, axis=-1, keepdims=True)).astype(jnp.bfloat16)
    mixed = jnp.einsum(
        "mhgqk,mkhd->mqhgd",
        weights.astype(jnp.float32),
        key_value_heads[:, :, :, 1],
        precision=lax.Precision.HIGHEST,
    )
    return mixed.reshape(batches * length, -1).astype(jnp.bfloat16)


def shards(tokens, queries, segment_ids, gain, key_value_weight, plan):
    rank_count = lax.axis_size("dp")
    own_rank = lax.axis_index("dp")
    batches = segment_ids.shape[0]
    length = segment_ids.shape[1]
    slot_cap = (batches + rank_count - 1) // rank_count
    dest_rank = plan.reshape(rank_count, batches) // batches
    slot_range = jnp.arange(batches, dtype=jnp.int32)
    same_dest = dest_rank[:, :, None] == dest_rank[:, None, :]
    earlier = slot_range[None, None, :] < slot_range[None, :, None]
    arrival = jnp.sum((same_dest & earlier).astype(jnp.int32), axis=2)
    own_dest = lax.dynamic_index_in_dim(dest_rank, own_rank, 0, keepdims=False)
    own_arrival = lax.dynamic_index_in_dim(arrival, own_rank, 0, keepdims=False)
    rank_range = jnp.arange(rank_count, dtype=jnp.int32)
    cap_range = jnp.arange(slot_cap, dtype=jnp.int32)
    send_hits = (
        (own_dest[None, None, :] == rank_range[:, None, None])
        & (own_arrival[None, None, :] == cap_range[None, :, None])
    ).astype(jnp.int32)
    send_index = jnp.sum(send_hits * slot_range[None, None, :], axis=2)
    send_valid = jnp.sum(send_hits, axis=2)
    inverse = jnp.argsort(plan)
    sources = lax.dynamic_slice_in_dim(inverse, own_rank * batches, batches)
    source_rank = sources // batches
    source_arrival = jnp.take(arrival.reshape(-1), sources)
    keep_index = source_rank * slot_cap + source_arrival
    local_kv = project(tokens, gain, key_value_weight)
    results = attend(queries, local_kv, segment_ids)
    parcel = pack_rows(send_index, send_valid, results.reshape(batches, -1), length)
    arrived = lax.all_to_all(parcel, "dp", split_axis=0, concat_axis=0, tiled=True)
    return unpack_rows(keep_index, arrived).reshape(batches * length, -1)


def solution(mesh):
    placed = (
        P(("dp", "fsdp"), "tensor"),
        P(("dp", "fsdp"), "tensor"),
        P(("dp", "fsdp"), None),
        P("tensor"),
        P("tensor", "fsdp"),
        P(),
    )
    return jax.shard_map(
        shards, mesh=mesh, in_specs=placed, out_specs=P(("dp", "fsdp"), "tensor"), check_vma=False
    )
```

profile of v0, /device:TPU:1, one launch (start us, length us, event | category | flops | bytes accessed | tf_op | source)
XLA Modules:
  0.0 254.4 jit_solution(3766419235261938822)
XLA Ops:
  6.5 0.7 all-gather.4.cloned.1.call-update
  7.3 1.2 fusion.4
  8.5 13.8 %all-gather.1 = f32[8,1,256]{2,1,0:T(1,128)S(1)} all-gather(f32[1,1,256]{2,1,0:T(1,128)S(1)} %bitcast.63), channel_id=2, replica_groups=mesh['dp'=16,'fsdp'=4,'tensor'=8] {'tensor'}, dimensions={0}, use_global_device_ids=true | all-gather | bytes 9216 | tf_op jit(solution)/shard_map/all_gather | solution.py:13
  22.4 46.1 %all-gather.4.cloned.1.call-done = bf16[1024,2048]{1,0:T(8,128)(2,1)} async-done(((bf16[1024,512]{1,0:T(8,128)(2,1)}), bf16[1024,2048]{1,0:T(8,128)(2,1)}) %all-gather.4.cloned.1.call-update) | async-done | bytes 4194320 | tf_op jit(solution)/shard_map/all_gather | solution.py:38
  68.5 5.0 %fusion.8 = f32[256,2048]{1,0:T(8,128)} fusion(bf16[1024,2048]{1,0:T(8,128)(2,1)} %all-gather.4.cloned.1.call-done, bf16[256,1024]{1,0:T(8,128)(2,1)} %param.6, f32[1024]{0:T(1024)} %param.9, f32[256]{0:T(256)S(1)} %add_rsqrt_fusion), kind=kOutput, calls=%fused_computation.21 | convolution fusion | flops 1074790400 | bytes 6820864 | tf_op jit(solution)/shard_map/dot_general | solution.py:36
  74.0 0.2 compare_reduce_fusion
  74.4 0.1 compare_and_fusion
  74.5 40.1 %reduce-scatter.2.cloned.1.call-done = f32[256,256]{1,0:T(8,128)} async-done(((f32[256,2048]{1,0:T(8,128)}), f32[256,256]{1,0:T(8,128)}) %reduce-scatter.2.cloned.1.call-update) | async-done | bytes 262160 | tf_op jit(solution)/shard_map/reduce_scatter | solution.py:41
  114.5 1.1 reshape.341
  115.6 0.2 fusion.21
  115.8 0.7 fusion.22
  116.5 0.2 fusion.7
  116.7 0.6 fusion.3
  117.3 0.3 copy.29
  117.6 0.1 convert_element_type.53
  117.8 0.4 fusion.20
  118.2 1.9 gather_fusion.1
  120.1 3.3 %gather_fusion.2 = bf16[16,65536]{1,0:T(8,128)(2,1)} fusion(bf16[2,65536]{1,0:T(2,128)(2,1)S(1)} %get-tuple-element.14, s32[1024]{0:T(1024)S(1)} %pad_clamp_fusion.1), kind=kCustom, calls=%fused_computation.2 | custom fusion | bytes 4194368 | tf_op jit(solution)/shard_map/jit(_take)/gather | solution.py:20
  123.4 1.9 pad_maximum_fusion
  125.3 2.3 copy.37
  127.6 2.6 %fusion = bf16[16,1,128,1024]{3,2,1,0:T(8,128)(2,1)} fusion(pred[16]{0:T(512)(128)(4,1)S(1)} %compare_and_fusion.1, bf16[16]{0:T(256)(128)(2,1)S(1)} %convert_element_type.55, bf16[2,8,128,1024]{3,2,1,0:T(8,128)(2,1)S(1)} %copy.37), kind=kLoop, calls=%fused_computation.7 | loop fusion | flops 4194304 | bytes 8388656 | tf_op jit(solution)/shard_map/mul | solution.py:21
  130.2 11.9 %all-to-all-start = ((bf16[16,1,128,1024]{3,2,1,0:T(8,128)(2,1)}), bf16[16,1,128,1024]{3,2,1,0:T(8,128)(2,1)}, u32[]{:S(2)}, u32[]{:S(2)}) async-start(bf16[16,1,128,1024]{3,2,1,0:T(8,128)(2,1)} %fusion), calls=%async_computation.1 | async-start | bytes 8388608 | tf_op jit(solution)/shard_map/all_to_all | solution.py:103
  142.2 1.6 sort.17
  144.0 0.6 gather_fusion
  144.8 90.9 %all-to-all-done = bf16[16,1,128,1024]{3,2,1,0:T(8,128)(2,1)} async-done(((bf16[16,1,128,1024]{3,2,1,0:T(8,128)(2,1)}), bf16[16,1,128,1024]{3,2,1,0:T(8,128)(2,1)}, u32[]{:S(2)}, u32[]{:S(2)}) %all-to-all-start) | async-done | bytes 4194336 | tf_op jit(solution)/shard_map/all_to_all | solution.py:103
  235.7 4.5 %copy.38 = bf16[2,8,128,1024]{3,1,2,0:T(8,128)(2,1)S(1)} copy(bf16[2,8,128,1024]{3,2,1,0:T(8,128)(2,1)} %bitcast.36) | data formatting | bytes 8388608
  240.2 1.6 fusion.19
  241.8 3.0 %gather_fusion.3 = bf16[2,65536]{1,0:T(2,128)(2,1)S(1)} fusion(bf16[16,65536]{1,0:T(8,128)(2,1)} %get-tuple-element.11, s32[1024]{0:T(1024)S(1)} %pad_clamp_fusion), kind=kCustom, calls=%fused_computation.3 | custom fusion | bytes 524296 | tf_op jit(solution)/shard_map/jit(_take)/gather | solution.py:27
  244.8 0.9 gather_fusion.4
  245.7 0.5 pad_maximum_fusion.1
  246.2 0.5 gather.20
  246.7 0.9 broadcast_select_fusion
  (32 shorter events, 1.0 us)
Async XLA Ops:
  6.5 62.0 %all-gather.4.cloned.1.call-start = ((), (), s32[]{:S(2)}) async-start(), calls=%async_computation.2 | async-start | bytes 5242880 | tf_op jit(solution)/shard_map/all_gather | solution.py:38
  7.3 107.3 %reduce-scatter.2.cloned.1.call-start = ((), (), s32[]{:S(2)}) async-start(), calls=%async_computation.3 | async-start | bytes 2359296 | tf_op jit(solution)/shard_map/reduce_scatter | solution.py:41
  22.4 51.2 %copy-start.2 = (s32[32]{0:T(128)S(1)}, s32[32]{0:T(128)}, u32[]{:S(2)}) copy-start(s32[32]{0:T(128)} %param.11) | copy-start | bytes 388
  22.4 51.4 %copy-start = (bf16[256,1024]{1,0:T(8,128)(2,1)S(1)}, bf16[256,1024]{1,0:T(8,128)(2,1)}, u32[]{:S(2)}) copy-start(bf16[256,1024]{1,0:T(8,128)(2,1)} %param.7) | copy-start | bytes 1572868
  22.4 51.9 %copy-start.1 = (s32[2,128]{1,0:T(2,128)S(1)}, s32[2,128]{1,0:T(2,128)}, u32[]{:S(2)}) copy-start(s32[2,128]{1,0:T(2,128)} %param.8) | copy-start | bytes 3076
  130.2 105.5 %all-to-all-start = ((bf16[16,1,128,1024]{3,2,1,0:T(8,128)(2,1)}), bf16[16,1,128,1024]{3,2,1,0:T(8,128)(2,1)}, u32[]{:S(2)}, u32[]{:S(2)}) async-start(bf16[16,1,128,1024]{3,2,1,0:T(8,128)(2,1)} %fusion), calls=%async_computation.1 | async-start | bytes 8388608 | tf_op jit(solution)/shard_map/all_to_all | solution.py:103
Sparse Core Ops, SparseCore 0:
  9.5 59.0 all-gather.3
  73.7 40.8 reduce-scatter.1
where the time goes:
time: 255 us; the launch traced here: 254 us
  waiting for transfers between devices  178 us (70%)
  local copies, waits for them, and re-layouts  21.3 us (8%)
  blocking collectives  13.8 us (5%)
  between operations  13.6 us (5%)
  starting transfers between devices  12 us (5%)
  other arithmetic  9.59 us (4%)
  matrix products  6.33 us (2%)
    all_to_all x1, waiting for transfers between devices, shards(): lax.all_to_all(parcel, 'dp', split_axis=0, concat_axis=0, tiled=True)  90.9 us
    all_gather x1, waiting for transfers between devices, project(): lax.all_gather(key_value_weight, 'fsdp', axis=1, tiled=True)  46.1 us
    reduce_scatter x1, waiting for transfers between devices, project(): lax.psum_scatter(partial_value, 'tensor', scatter_dimension=1, tiled=True)  40.1 us
    all_gather x1, blocking collectives, total_of_pieces(): parts = lax.all_gather(array, axis)  13.8 us
    all_to_all x1, starting transfers between devices, shards(): lax.all_to_all(parcel, 'dp', split_axis=0, concat_axis=0, tiled=True)  11.9 us
    unnamed x9, local copies, waits for them, and re-layouts  6.94 us
    gather x4, local copies, waits for them, and re-layouts, unpack_rows(): return jnp.take(flat, keep_index, axis=0)  5.95 us
    gather x3, local copies, waits for them, and re-layouts, pack_rows(): taken = jnp.take(flat_rows, send_index.reshape(-1), axis=0)  5.59 us
  transfers between devices with their start and end apart: 3, of which 3 were waited for; matrix products, arithmetic and copies ran while one was open for 2% of the time, Pallas kernels for 0%

commit v1 on v0

v1 whole, which is shorter than its diff:
```python
import functools
import jax
import jax.numpy as jnp
from jax import lax
from jax.experimental import pallas as pl
from jax.experimental.pallas import tpu as pltpu
from jax.sharding import PartitionSpec as P

HEAD_SIZE = 128
EPSILON = 1e-05
VMEM = pl.BlockSpec(memory_space=pltpu.VMEM)
SMEM = pl.BlockSpec(memory_space=pltpu.SMEM)


def call(kernel, out_shape, in_specs, scratch, flops, moved, limit=24 << 20):
    return pl.pallas_call(
        kernel,
        out_shape=out_shape,
        in_specs=in_specs,
        out_specs=jax.tree.map(lambda _: VMEM, out_shape),
        scratch_shapes=scratch,
        compiler_params=pltpu.CompilerParams(vmem_limit_bytes=limit),
        cost_estimate=pl.CostEstimate(flops=flops, bytes_accessed=moved, transcendentals=0),
    )


def place_queries_kernel(plan, arrived, out, stage):
    ranks = arrived.shape[0]
    for p in range(ranks):
        rows = arrived[p, 16:32, :].astype(jnp.float32)
        for s in range(2):
            stage[pl.ds(pl.multiple_of(plan[2 * p + s] * 8, 8), 8), :] = rows[s * 8:s * 8 + 8]
    out[...] = stage[...].astype(jnp.bfloat16).reshape(out.shape)


def project_kernel(plan, place, arrived, scale, gain, own, right, left, far_a, far_b,
                   right_o, left_o, far_ao, far_bo, out, stage, normed):
    ranks = arrived.shape[0]
    half = normed.shape[2]
    quarter = half // 2
    for p in range(ranks):
        rows = arrived[p, 0:16, :].astype(jnp.float32)
        rows = rows * scale[p * 16:p * 16 + 16, :] * gain[...]
        for s in range(2):
            stage[pl.ds(pl.multiple_of(plan[2 * p + s] * 8, 8), 8), :] = rows[s * 8:s * 8 + 8]
    for i in range(2):
        normed[i] = stage[:, i * half:(i + 1) * half].astype(jnp.bfloat16)
    core = place[0]
    shard = place[1]

    def dot(a, b):
        return jnp.dot(a, b, preferred_element_type=jnp.float32)

    def put(index, total):
        blocks = total.astype(jnp.bfloat16).reshape(ranks, 16, 2 * 2 * HEAD_SIZE)
        for h in range(2):
            out[:, index * 2 + h] = blocks[:, :, h * 2 * HEAD_SIZE:(h + 1) * 2 * HEAD_SIZE]

    put(shard, dot(normed[0], own[:half, :]) + dot(normed[1], own[half:, :]))
    mine, other = normed.at[core], normed.at[1 - core]
    put(lax.rem(shard + 3, 4), dot(mine[...], right[...]) + dot(other[...], right_o[...]))
    put(lax.rem(shard + 1, 4), dot(mine[...], left[...]) + dot(other[...], left_o[...]))
    put(
        lax.rem(shard + 2, 4),
        dot(mine[:, :quarter], far_a[...]) + dot(mine[:, quarter:], far_b[...])
        + dot(other[:, :quarter], far_ao[...]) + dot(other[:, quarter:], far_bo[...]),
    )


def attend_kernel(parts, queries, seg_row, seg_col, out, key_value):
    groups = 8
    ranks = queries.shape[0]
    length = key_value.shape[1]
    for i in range(ranks):
        total = parts[i * groups].astype(jnp.float32)
        for k in range(1, groups):
            total = total + parts[i * groups + k].astype(jnp.float32)
        for s in range(2):
            key_value[s, i * 8:i * 8 + 8, :] = total[s * 8:s * 8 + 8]
    rows = lax.broadcasted_iota(jnp.int32, (length, length), 0)
    columns = lax.broadcasted_iota(jnp.int32, (length, length), 1)
    wide = queries[...].astype(jnp.float32).reshape(ranks, 2, 8, queries.shape[2])
    for s in range(2):
        allowed = (seg_col[s * length:(s + 1) * length, :] == seg_row[s:s + 1, :]) & (columns <= rows)
        key = key_value[s, :, :HEAD_SIZE]
        value = key_value[s, :, HEAD_SIZE:]
        key_high = key.astype(jnp.bfloat16)
        key_low = (key - key_high.astype(jnp.float32)).astype(jnp.bfloat16)
        value_high = value.astype(jnp.bfloat16)
        value_low = (value - value_high.astype(jnp.float32)).astype(jnp.bfloat16)
        query = wide[:, s].reshape(length, queries.shape[2]).astype(jnp.bfloat16)
        for n in range(groups):
            at = query[:, n * HEAD_SIZE:(n + 1) * HEAD_SIZE]
            turned = (((1,), (1,)), ((), ()))
            scores = lax.dot_general(at, key_high, turned, preferred_element_type=jnp.float32)
            scores = scores + lax.dot_general(at, key_low, turned, preferred_element_type=jnp.float32)
            scores = jnp.where(allowed, scores * HEAD_SIZE ** (-0.5), -1e30)
            expo = jnp.exp(scores - jnp.max(scores, axis=1, keepdims=True))
            weights = (expo / jnp.sum(expo, axis=1, keepdims=True)).astype(jnp.bfloat16)
            mixed = jnp.dot(weights, value_high, preferred_element_type=jnp.float32)
            mixed = mixed + jnp.dot(weights, value_low, preferred_element_type=jnp.float32)
            out[s * length:(s + 1) * length, n * HEAD_SIZE:(n + 1) * HEAD_SIZE] = mixed.astype(jnp.bfloat16)


def gather_weight(weight, core):
    half = weight.shape[0] // 2
    up = [(i, (i + 1) % 4) for i in range(4)]
    down = [(i, (i + 3) % 4) for i in range(4)]
    swap = [(i, i ^ 1) for i in range(16)]
    mine = lax.dynamic_slice_in_dim(weight, core * half, half, 0)
    right = lax.ppermute(mine, "fsdp", up)
    left = lax.ppermute(mine, "fsdp", down)
    far_a = lax.ppermute(right[:half // 2], "fsdp", up)
    far_b = lax.ppermute(left[half // 2:], "fsdp", down)
    held = (right, left, far_a, far_b)
    return held + tuple(lax.ppermute(a, "dp", swap) for a in held)


def shards(tokens, queries, segment_ids, gain, weight, plan):
    ranks = lax.axis_size("dp")
    groups = lax.axis_size("tensor")
    rank = lax.axis_index("dp")
    width = tokens.shape[1]
    slots, length = segment_ids.shape
    core = lax.rem(rank, 2)
    place = jnp.stack([core, lax.axis_index("fsdp")]).astype(jnp.int32)

    def cut(a):
        return a.reshape(slots, ranks, 8, width).transpose(1, 0, 2, 3)

    first = jnp.concatenate([cut(tokens), cut(queries)], axis=1)
    arrived = lax.all_to_all(first, "dp", 0, 0, tiled=True).reshape(ranks, 32, width)
    pieces = gather_weight(weight, core)

    values = tokens.astype(jnp.float32)
    sums = jnp.sum(values * values, axis=1).reshape(slots, length)
    facts = jnp.stack([sums, segment_ids.astype(jnp.float32)])
    facts = lax.all_gather(facts, ("dp", "tensor")).reshape(ranks, groups, 2, slots, length)
    totals = facts[:, :, 0].sum(axis=1).reshape(ranks * slots, length)
    scale = lax.rsqrt(totals / (width * groups) + EPSILON)
    scale = lax.dynamic_slice_in_dim(scale, rank * 8, 8, 1).reshape(ranks * slots * 8, 1)
    goal = rank * slots + jnp.arange(slots, dtype=jnp.int32)
    here = (plan[None, :] == goal[:, None]).astype(jnp.float32)
    documents = facts[:, 0, 1].reshape(ranks * slots, length)
    documents = (here[:, :, None] * documents[None]).sum(axis=1)

    placed = call(
        place_queries_kernel,
        jax.ShapeDtypeStruct((ranks, 16, width), jnp.bfloat16),
        [SMEM, VMEM],
        [pltpu.VMEM((ranks * 16, width), jnp.float32)],
        0, 2 << 20,
    )(plan, arrived)
    placed = lax.all_to_all(placed, "dp", 0, 0, tiled=True)

    rows = ranks * 16
    parts = call(
        project_kernel,
        jax.ShapeDtypeStruct((ranks, groups, 16, 2 * HEAD_SIZE), jnp.bfloat16),
        [SMEM, SMEM] + [VMEM] * 12,
        [pltpu.VMEM((rows, width), jnp.float32), pltpu.VMEM((2, rows, width // 2), jnp.bfloat16)],
        2 * rows * width * groups * 2 * HEAD_SIZE, 8 << 20,
    )(plan, place, arrived, scale, gain.reshape(1, width), weight, *pieces)
    parts = lax.all_to_all(
        parts.reshape(ranks * groups, 16, 2 * HEAD_SIZE), ("dp", "tensor"), 0, 0, tiled=True
    )

    return call(
        attend_kernel,
        jax.ShapeDtypeStruct((slots * length, width), jnp.bfloat16),
        [VMEM] * 4,
        [pltpu.VMEM((slots, length, 2 * HEAD_SIZE), jnp.float32)],
        8 * slots * 8 * length * length * HEAD_SIZE, 4 << 20,
    )(parts, placed, documents, documents.reshape(slots * length, 1))


def solution(mesh):
    placed = (
        P(("dp", "fsdp"), "tensor"),
        P(("dp", "fsdp"), "tensor"),
        P(("dp", "fsdp"), None),
        P("tensor"),
        P("tensor", "fsdp"),
        P(),
    )
    return jax.shard_map(
        shards, mesh=mesh, in_specs=placed, out_specs=P(("dp", "fsdp"), "tensor"), check_vma=False
    )
```

time: 255 us -> 210 us (0.82)
  waiting for transfers between devices: 178 us -> 49.8 us
  blocking collectives: 13.8 us -> 89 us
  starting transfers between devices: 12 us -> 49.2 us
  local copies, waits for them, and re-layouts: 21.3 us -> 5.78 us
  between operations: 13.6 us -> 0.24 us
  Pallas kernels: 0 us -> 12.4 us
  other arithmetic: 9.59 us -> 2.63 us
  matrix products: 6.33 us -> 0 us
    all_gather x1, blocking collectives: 13.8 us -> 89 us  [shards(): lax.all_gather(facts, ('dp', 'tensor'))]
    all_gather x1 -> x0, waiting for transfers between devices: 46.1 us -> none  [project(): lax.all_gather(key_value_weight, 'fsdp', axis=1, tiled=True)]
    all_to_all x1 -> x3, waiting for transfers between devices: 90.9 us -> 49.6 us  [the longest x1 29 us: shards(): lax.all_to_all(parts.reshape(ranks * groups, 16, 2 * HEAD_SIZE), ('dp', '...]
    reduce_scatter x1 -> x0, waiting for transfers between devices: 40.1 us -> none  [project(): lax.psum_scatter(partial_value, 'tensor', scatter_dimension=1, tiled=True)]
    ppermute x0 -> x8, starting transfers between devices: none -> 22.6 us  [the longest x4 9.55 us: gather_weight(): return held + tuple((lax.ppermute(a, 'dp', swap) for a in held))]
    all_to_all x1 -> x3, starting transfers between devices: 11.9 us -> 26.6 us  [the longest x1 12 us: shards(): lax.all_to_all(first, 'dp', 0, 0, tiled=True).reshape(ranks, 32, width)]
    pallas_call x0 -> x3, Pallas kernels: none -> 12.4 us  [the longest x1 6.94 us: shards(): call(attend_kernel, jax.ShapeDtypeStruct((slots * length, width), jnp.bfl...]
    gather x8 -> x0, local copies, waits for them, and re-layouts: 12.2 us -> none  [the longest x4 5.95 us: unpack_rows(): return jnp.take(flat, keep_index, axis=0)]
  transfers between devices with their start and end apart: 3 -> 11, of which waited for: 3 -> 3; matrix products, arithmetic and copies ran while one was open for 2% -> 3% of each run, Pallas kernels for 0% -> 3%
where the time goes in v1:
time: 210 us; the launch traced here: 209 us
  blocking collectives  89 us (42%)
  waiting for transfers between devices  49.8 us (24%)
  starting transfers between devices  49.2 us (23%)
  Pallas kernels  12.4 us (6%)
  local copies, waits for them, and re-layouts  5.78 us (3%)
  other arithmetic  2.63 us (1%)
    all_gather x1, blocking collectives, shards(): lax.all_gather(facts, ('dp', 'tensor'))  89 us
    all_to_all x1, waiting for transfers between devices, shards(): lax.all_to_all(parts.reshape(ranks * groups, 16, 2 * HEAD_SIZE), ('dp', '...  29 us
    all_to_all x1, waiting for transfers between devices, shards(): lax.all_to_all(first, 'dp', 0, 0, tiled=True).reshape(ranks, 32, width)  20.6 us
    all_to_all x1, starting transfers between devices, shards(): lax.all_to_all(first, 'dp', 0, 0, tiled=True).reshape(ranks, 32, width)  12 us
    all_to_all x1, starting transfers between devices, shards(): lax.all_to_all(parts.reshape(ranks * groups, 16, 2 * HEAD_SIZE), ('dp', '...  11.2 us
    ppermute x4, starting transfers between devices, gather_weight(): return held + tuple((lax.ppermute(a, 'dp', swap) for a in held))  9.55 us
    pallas_call x1, Pallas kernels, shards(): call(attend_kernel, jax.ShapeDtypeStruct((slots * length, width), jnp.bfl...  6.94 us
  transfers between devices with their start and end apart: 11, of which 3 were waited for; matrix products, arithmetic and copies ran while one was open for 3% of the time, Pallas kernels for 3%

profile of v1, /device:TPU:1, one launch (start us, length us, event | category | flops | bytes accessed | tf_op | source)
XLA Modules:
  0.0 209.1 jit_solution(1845443233694375781)
XLA Ops:
  0.0 1.1 copy.23
  1.1 0.1 copy-done.3
  1.2 1.1 pad_maximum_fusion
  2.3 12.0 %all-to-all-start = ((bf16[16,4,8,1024]{3,2,1,0:T(8,128)(2,1)}), bf16[16,4,8,1024]{3,2,1,0:T(8,128)(2,1)S(1)}, u32[]{:S(2)}, u32[]{:S(2)}) async-start(bf16[16,4,8,1024]{3,2,1,0:T(8,128)(2,1)} %pad_maximum_fusion), calls=%async_computation | async-start | bytes 2097152 | tf_op jit(solution)/shard_map/all_to_all | solution.py:132
  14.3 0.8 constant_dynamic-slice_fusion
  15.2 3.1 %collective-permute-start = (bf16[512,512]{1,0:T(8,128)(2,1)}, bf16[512,512]{1,0:T(8,128)(2,1)S(1)}, u32[]{:S(2)}, u32[]{:S(2)}) collective-permute-start(bf16[512,512]{1,0:T(8,128)(2,1)} %constant_dynamic-slice_fusion), channel_id=1, source_target_pairs={{0,8},{8,16},{16,24},{24,0},{1,9},{9,17},{17,25},{25,1},{2,10},{10... | collective-permute-start | bytes 1572872 | tf_op jit(solution)/shard_map/ppermute | solution.py:111
  18.3 3.4 %collective-permute-start.1 = (bf16[512,512]{1,0:T(8,128)(2,1)}, bf16[512,512]{1,0:T(8,128)(2,1)}, u32[]{:S(2)}, u32[]{:S(2)}) collective-permute-start(bf16[512,512]{1,0:T(8,128)(2,1)} %constant_dynamic-slice_fusion), channel_id=1, source_target_pairs={{0,24},{8,0},{16,8},{24,16},{1,25},{9,1},{17,9},{25,17},{2,26},{10... | collective-permute-start | bytes 1572872 | tf_op jit(solution)/shard_map/ppermute | solution.py:112
  21.7 20.6 %all-to-all-done = bf16[16,4,8,1024]{3,2,1,0:T(8,128)(2,1)S(1)} async-done(((bf16[16,4,8,1024]{3,2,1,0:T(8,128)(2,1)}), bf16[16,4,8,1024]{3,2,1,0:T(8,128)(2,1)S(1)}, u32[]{:S(2)}, u32[]{:S(2)}) %all-to-all-start) | async-done | bytes 1048608 | tf_op jit(solution)/shard_map/all_to_all | solution.py:132
  42.2 1.5 shard_map.65
  43.7 3.5 %all-to-all-start.2 = ((bf16[16,16,1024]{2,1,0:T(8,128)(2,1)}), bf16[16,16,1024]{2,1,0:T(8,128)(2,1)S(1)}, u32[]{:S(2)}, u32[]{:S(2)}) async-start(bf16[16,16,1024]{2,1,0:T(8,128)(2,1)} %shard_map.65), calls=%async_computation.2 | async-start | bytes 1048576 | tf_op jit(solution)/shard_map/all_to_all | solution.py:154
  47.2 1.2 multiply_reduce_fusion
  48.5 3.1 %collective-permute-start.2 = (bf16[256,512]{1,0:T(8,128)(2,1)S(1)}, bf16[256,512]{1,0:T(8,128)(2,1)S(1)}, u32[]{:S(2)}, u32[]{:S(2)}) collective-permute-start(bf16[256,512]{1,0:T(8,128)(2,1)S(1)} %slice.17), channel_id=1, source_target_pairs={{0,8},{8,16},{16,24},{24,0},{1,9},{9,17},{17,25},{25,1},{2,10},{10... | collective-permute-start | bytes 786440 | tf_op jit(solution)/shard_map/ppermute | solution.py:113
  51.6 1.0 slice.18
  52.6 3.4 %collective-permute-start.3 = (bf16[256,512]{1,0:T(8,128)(2,1)S(1)}, bf16[256,512]{1,0:T(8,128)(2,1)}, u32[]{:S(2)}, u32[]{:S(2)}) collective-permute-start(bf16[256,512]{1,0:T(8,128)(2,1)S(1)} %slice.18), channel_id=1, source_target_pairs={{0,24},{8,0},{16,8},{24,16},{1,25},{9,1},{17,9},{25,17},{2,26},{10... | collective-permute-start | bytes 786440 | tf_op jit(solution)/shard_map/ppermute | solution.py:114
  56.0 89.0 %all-gather = f32[256,2,128]{2,1,0:T(2,128)S(1)} all-gather(f32[2,2,128]{2,1,0:T(2,128)S(1)} %pad_maximum_fusion.1), channel_id=2, replica_groups=mesh['dp'=16,'fsdp'=4,'tensor'=8] {'dp','tensor'}, dimensions={0}, use_global_device_ids=true | all-gather | bytes 264192 | tf_op jit(solution)/shard_map/all_gather | solution.py:138
  145.0 3.3 %collective-permute-start.4 = (bf16[512,512]{1,0:T(8,128)(2,1)S(1)}, bf16[512,512]{1,0:T(8,128)(2,1)}, u32[]{:S(2)}, u32[]{:S(2)}) collective-permute-start(bf16[512,512]{1,0:T(8,128)(2,1)S(1)} %collective-permute-done.right), channel_id=1, source_target_pairs={{0,32},{32,0},{64,96},{96,64},{128,160},{160,128},{192,224},{224,1... | collective-permute-start | bytes 1572872 | tf_op jit(solution)/shard_map/ppermute | solution.py:116
  148.3 1.9 collective-permute-start.5
  150.3 2.4 %collective-permute-start.6 = (bf16[256,512]{1,0:T(8,128)(2,1)S(1)}, bf16[256,512]{1,0:T(8,128)(2,1)}, u32[]{:S(2)}, u32[]{:S(2)}) collective-permute-start(bf16[256,512]{1,0:T(8,128)(2,1)S(1)} %collective-permute-done.2.far_a), channel_id=1, source_target_pairs={{0,32},{32,0},{64,96},{96,64},{128,160},{160,128},{192,224},{224,1... | collective-permute-start | bytes 786440 | tf_op jit(solution)/shard_map/ppermute | solution.py:116
  152.8 1.9 collective-permute-start.7
  154.7 0.7 constant_dynamic-slice_fusion.1
  155.4 0.8 reshape.72.scale
  156.2 0.1 pad_add_fusion.place
  156.3 0.2 collective-permute-done.7.far_bo
  156.5 0.4 copy-done.2
  156.9 4.0 %shard_map.64 = bf16[16,8,16,256]{3,2,1,0:T(8,128)(2,1)} custom-call(s32[32]{0:T(128)S(1)} %copy-done.1, s32[2]{0:T(128)S(1)} %pad_add_fusion.place, bf16[16,32,1024]{2,1,0:T(8,128)(2,1)S(1)} %bitcast.21, f32[256,1]{1,0:T(8,128)S(1)} %reshape.72.scale, f32[1,1024]{1,0:T(1,128)S(1)} %bitcast.23, bf16[1024,512]{1,0:T(8,128)(2,1)S(1)} %copy-done, ...), custom_call_target="tpu_custom_call" | custom-call | flops 1073741824 | bytes 8388608 | tf_op jit(solution)/shard_map/pallas_call | solution.py:157
  160.9 11.2 %all-to-all-start.1 = ((bf16[128,16,256]{2,1,0:T(8,128)(2,1)}), bf16[128,16,256]{2,1,0:T(8,128)(2,1)S(1)}, u32[]{:S(2)}, u32[]{:S(2)}) async-start(bf16[128,16,256]{2,1,0:T(8,128)(2,1)} %bitcast.12), calls=%async_computation.1 | async-start | bytes 2097152 | tf_op jit(solution)/shard_map/all_to_all | solution.py:164
  172.1 0.7 slice.19
  172.8 0.1 compare_convert_fusion
  172.9 0.1 multiply_reduce_fusion.1.seg_row
  173.0 0.1 copy.20.seg_col
  173.1 29.0 %all-to-all-done.1.parts = bf16[128,16,256]{2,1,0:T(8,128)(2,1)S(1)} async-done(((bf16[128,16,256]{2,1,0:T(8,128)(2,1)}), bf16[128,16,256]{2,1,0:T(8,128)(2,1)S(1)}, u32[]{:S(2)}, u32[]{:S(2)}) %all-to-all-start.1) | async-done | bytes 1048608 | tf_op jit(solution)/shard_map/all_to_all | solution.py:164
  202.1 6.9 %shard_map.66 = bf16[256,1024]{1,0:T(8,128)(2,1)} custom-call(bf16[128,16,256]{2,1,0:T(8,128)(2,1)S(1)} %all-to-all-done.1.parts, bf16[16,16,1024]{2,1,0:T(8,128)(2,1)S(1)} %all-to-all-done.2.queries, f32[2,128]{1,0:T(2,128)S(1)} %multiply_reduce_fusion.1.seg_row, f32[256,1]{1,0:T(8,128)S(1)} %copy.20.seg_col), custom_call_target="tpu_custom_call" | custom-call | flops 268435456 | bytes 4194304 | tf_op jit(solution)/shard_map/pallas_call | solution.py:168
  (25 shorter events, 0.2 us)
Async XLA Ops:
  0.0 1.2 copy-start.3
  2.3 12.0 %copy-start = (bf16[1024,512]{1,0:T(8,128)(2,1)S(1)}, bf16[1024,512]{1,0:T(8,128)(2,1)}, u32[]{:S(2)}) copy-start(bf16[1024,512]{1,0:T(8,128)(2,1)} %own.1) | copy-start | bytes 3145732
  2.3 39.9 %all-to-all-start = ((bf16[16,4,8,1024]{3,2,1,0:T(8,128)(2,1)}), bf16[16,4,8,1024]{3,2,1,0:T(8,128)(2,1)S(1)}, u32[]{:S(2)}, u32[]{:S(2)}) async-start(bf16[16,4,8,1024]{3,2,1,0:T(8,128)(2,1)} %pad_maximum_fusion), calls=%async_computation | async-start | bytes 2097152 | tf_op jit(solution)/shard_map/all_to_all | solution.py:132
  14.3 7.3 %copy-start.5 = (s32[2,128]{1,0:T(2,128)S(1)}, s32[2,128]{1,0:T(2,128)}, u32[]{:S(2)}) copy-start(s32[2,128]{1,0:T(2,128)} %param.8) | copy-start | bytes 3076
  15.2 33.3 %collective-permute-start = (bf16[512,512]{1,0:T(8,128)(2,1)}, bf16[512,512]{1,0:T(8,128)(2,1)S(1)}, u32[]{:S(2)}, u32[]{:S(2)}) collective-permute-start(bf16[512,512]{1,0:T(8,128)(2,1)} %constant_dynamic-slice_fusion), channel_id=1, source_target_pairs={{0,8},{8,16},{16,24},{24,0},{1,9},{9,17},{17,25},{25,1},{2,10},{10... | collective-permute-start | bytes 1572872 | tf_op jit(solution)/shard_map/ppermute | solution.py:111
  18.3 33.4 %collective-permute-start.1 = (bf16[512,512]{1,0:T(8,128)(2,1)}, bf16[512,512]{1,0:T(8,128)(2,1)}, u32[]{:S(2)}, u32[]{:S(2)}) collective-permute-start(bf16[512,512]{1,0:T(8,128)(2,1)} %constant_dynamic-slice_fusion), channel_id=1, source_target_pairs={{0,24},{8,0},{16,8},{24,16},{1,25},{9,1},{17,9},{25,17},{2,26},{10... | collective-permute-start | bytes 1572872 | tf_op jit(solution)/shard_map/ppermute | solution.py:112
  21.7 20.6 %copy-start.1 = (s32[32]{0:T(128)S(1)}, s32[32]{0:T(128)}, u32[]{:S(2)}) copy-start(s32[32]{0:T(128)} %plan.3) | copy-start | bytes 388
  43.7 117.2 %all-to-all-start.2 = ((bf16[16,16,1024]{2,1,0:T(8,128)(2,1)}), bf16[16,16,1024]{2,1,0:T(8,128)(2,1)S(1)}, u32[]{:S(2)}, u32[]{:S(2)}) async-start(bf16[16,16,1024]{2,1,0:T(8,128)(2,1)} %shard_map.65), calls=%async_computation.2 | async-start | bytes 1048576 | tf_op jit(solution)/shard_map/all_to_all | solution.py:154
  48.5 101.8 %collective-permute-start.2 = (bf16[256,512]{1,0:T(8,128)(2,1)S(1)}, bf16[256,512]{1,0:T(8,128)(2,1)S(1)}, u32[]{:S(2)}, u32[]{:S(2)}) collective-permute-start(bf16[256,512]{1,0:T(8,128)(2,1)S(1)} %slice.17), channel_id=1, source_target_pairs={{0,8},{8,16},{16,24},{24,0},{1,9},{9,17},{17,25},{25,1},{2,10},{10... | collective-permute-start | bytes 786440 | tf_op jit(solution)/shard_map/ppermute | solution.py:113
  52.6 100.2 %collective-permute-start.3 = (bf16[256,512]{1,0:T(8,128)(2,1)S(1)}, bf16[256,512]{1,0:T(8,128)(2,1)}, u32[]{:S(2)}, u32[]{:S(2)}) collective-permute-start(bf16[256,512]{1,0:T(8,128)(2,1)S(1)} %slice.18), channel_id=1, source_target_pairs={{0,24},{8,0},{16,8},{24,16},{1,25},{9,1},{17,9},{25,17},{2,26},{10... | collective-permute-start | bytes 786440 | tf_op jit(solution)/shard_map/ppermute | solution.py:114
  145.0 5.3 %copy-start.4 = (f32[256,2,128]{2,1,0:T(2,128)}, f32[256,2,128]{2,1,0:T(2,128)S(1)}, u32[]{:S(2)}) copy-start(f32[256,2,128]{2,1,0:T(2,128)S(1)} %all-gather) | copy-start | bytes 786436
  145.0 11.3 %collective-permute-start.4 = (bf16[512,512]{1,0:T(8,128)(2,1)S(1)}, bf16[512,512]{1,0:T(8,128)(2,1)}, u32[]{:S(2)}, u32[]{:S(2)}) collective-permute-start(bf16[512,512]{1,0:T(8,128)(2,1)S(1)} %collective-permute-done.right), channel_id=1, source_target_pairs={{0,32},{32,0},{64,96},{96,64},{128,160},{160,128},{192,224},{224,1... | collective-permute-start | bytes 1572872 | tf_op jit(solution)/shard_map/ppermute | solution.py:116
  148.3 8.0 %collective-permute-start.5 = (bf16[512,512]{1,0:T(8,128)(2,1)}, bf16[512,512]{1,0:T(8,128)(2,1)}, u32[]{:S(2)}, u32[]{:S(2)}) collective-permute-start(bf16[512,512]{1,0:T(8,128)(2,1)} %collective-permute-done.1.left), channel_id=1, source_target_pairs={{0,32},{32,0},{64,96},{96,64},{128,160},{160,128},{192,224},{224,1... | collective-permute-start | bytes 1572872 | tf_op jit(solution)/shard_map/ppermute | solution.py:116
  150.3 6.0 %collective-permute-start.6 = (bf16[256,512]{1,0:T(8,128)(2,1)S(1)}, bf16[256,512]{1,0:T(8,128)(2,1)}, u32[]{:S(2)}, u32[]{:S(2)}) collective-permute-start(bf16[256,512]{1,0:T(8,128)(2,1)S(1)} %collective-permute-done.2.far_a), channel_id=1, source_target_pairs={{0,32},{32,0},{64,96},{96,64},{128,160},{160,128},{192,224},{224,1... | collective-permute-start | bytes 786440 | tf_op jit(solution)/shard_map/ppermute | solution.py:116
  152.8 3.8 %collective-permute-start.7 = (bf16[256,512]{1,0:T(8,128)(2,1)}, bf16[256,512]{1,0:T(8,128)(2,1)}, u32[]{:S(2)}, u32[]{:S(2)}) collective-permute-start(bf16[256,512]{1,0:T(8,128)(2,1)} %collective-permute-done.3.far_b), channel_id=1, source_target_pairs={{0,32},{32,0},{64,96},{96,64},{128,160},{160,128},{192,224},{224,1... | collective-permute-start | bytes 786440 | tf_op jit(solution)/shard_map/ppermute | solution.py:116
  156.2 0.7 copy-start.2
  160.9 41.2 %all-to-all-start.1 = ((bf16[128,16,256]{2,1,0:T(8,128)(2,1)}), bf16[128,16,256]{2,1,0:T(8,128)(2,1)S(1)}, u32[]{:S(2)}, u32[]{:S(2)}) async-start(bf16[128,16,256]{2,1,0:T(8,128)(2,1)} %bitcast.12), calls=%async_computation.1 | async-start | bytes 2097152 | tf_op jit(solution)/shard_map/all_to_all | solution.py:164
